TPU v7x, 32 devices: a whole 2x2x4 slice. The times are simulated.
32 devices in a mesh: src: 8 (over z, x), tgt: 4 (over y, core).
Axes of the slice: x: 2, y: 2, z: 4, core: 2. Of those that a mesh axis runs over, the one named last changes fastest.
Arguments:
- src_feat: bfloat16 [16384, 768], P(('src', 'tgt')), may hold values from -6 to 6
- tgt_feat: bfloat16 [8192, 768], P(('tgt', 'src')), may hold values from -6 to 6
- rel_weight: bfloat16 [3, 768, 1024], replicated, may hold values from -0.21875 to 0.21875
- self_weight: bfloat16 [768, 1024], replicated, may hold values from -0.21875 to 0.21875
- adj_weight: bfloat16 [8, 64, 4, 128, 128], P('src', 'tgt'), may hold values from 0 to 0.026977539
- adj_source: int32 [8, 64, 4], P('src', 'tgt'), may hold values from 0 to 47
- adj_count: int32 [8, 64], P('src', 'tgt'), may hold values from 1 to 4
Outputs:
- hidden_out: bfloat16 [8192, 1024], P(('tgt', 'src'))
All inputs are finite; a program needn't handle non-finite values.
Results may differ from a plain program's by a relative error of at most 0.004.
Values may be sent and summed in bfloat16 or wider, within the bound.
A program may use at most 128 MiB of HBM per device.

v0:
```python
import jax
import jax.numpy as jnp
from jax import lax
from jax.sharding import PartitionSpec as P

HID = 1024
BLK = 128


def shards(src_feat, tgt_feat, rel_weight, self_weight, adj_weight, adj_source, adj_count):
    gathered = lax.all_gather(src_feat, "tgt", axis=0, tiled=True)
    transformed = jnp.einsum(
        "nd,rdh->rnh", gathered, rel_weight, preferred_element_type=jnp.float32
    ).astype(jnp.bfloat16)
    blocks_all = transformed.shape[0] * (transformed.shape[1] // BLK)
    transformed = transformed.reshape(blocks_all, BLK, HID)
    weights = adj_weight[0]
    source_index = adj_source[0]
    count_live = adj_count[0]
    tblocks = weights.shape[0]
    slots = weights.shape[1]
    slot_iota = jnp.arange(slots, dtype=jnp.int32)
    alive_mask = slot_iota[None, :] < count_live[:, None]
    live_weight = jnp.where(alive_mask[:, :, None, None], weights, jnp.zeros_like(weights))
    live_weight = jnp.transpose(live_weight, (0, 2, 1, 3)).reshape(tblocks, BLK, slots * BLK)
    picked = jnp.take(transformed, source_index.reshape(-1), axis=0).reshape(
        tblocks, slots * BLK, HID
    )
    partial_value = jnp.einsum(
        "tij,tjh->tih", live_weight, picked, preferred_element_type=jnp.float32
    )
    partial_value = partial_value.reshape(tblocks * BLK, HID)
    summed = lax.psum_scatter(partial_value, "src", scatter_dimension=0, tiled=True)
    self_term = jnp.dot(tgt_feat, self_weight, preferred_element_type=jnp.float32)
    return jax.nn.relu(summed + self_term).astype(jnp.bfloat16)


def solution(mesh):
    return jax.shard_map(
        shards,
        mesh=mesh,
        in_specs=(
            P(("src", "tgt"), None),
            P(("tgt", "src"), None),
            P(),
            P(),
            P("src", "tgt", None, None, None),
            P("src", "tgt", None),
            P("src", "tgt"),
        ),
        out_specs=P(("tgt", "src"), None),
        check_vma=False,
    )
```

profile of v0, /device:TPU:0, one launch (start us, length us, event | category | flops | bytes accessed | tf_op | source)
XLA Modules:
  0.0 259.3 jit_solution(10372523398041055060)
XLA Ops:
  6.5 0.0 copy-start
  6.5 0.0 copy-start.2
  6.5 0.0 all-gather.2.cloned.1.call-start
  6.5 0.7 all-gather.2.cloned.1.call-update
  7.3 0.0 reduce-scatter.2.cloned.1.call-start
  7.3 0.8 copy.15
  8.1 0.1 reshape_squeeze.6
  8.2 0.7 compare_and_fusion
  8.8 0.1 copy.12
  9.0 0.1 broadcast_in_dim.29
  9.1 3.9 %copy.11 = bf16[1,16,4,128,128]{3,4,2,1,0:T(8,128)(2,1)} copy(bf16[1,16,4,128,128]{4,3,2,1,0:T(8,128)(2,1)} %param.11) | data formatting | bytes 4194304 | tf_op args[4]
  13.0 0.0 copy-done.2
  13.0 0.1 iota_compare_fusion
  13.1 3.1 %bitcast_select_fusion.1 = bf16[16,4,128,128]{2,3,1,0:T(8,128)(2,1)} fusion(bf16[1,16,4,128,128]{3,4,2,1,0:T(8,128)(2,1)} %copy.11, pred[16,4]{1,0:T(8,128)(4,1)S(1)} %iota_compare_fusion), kind=kLoop, calls=%fused_computation.4 | loop fusion | flops 1048576 | bytes 4194368 | tf_op jit(solution)/shard_map/jit(_where)/select_n | solution.py:24
  16.2 24.0 %all-gather.2.cloned.1.call-done = bf16[2048,768]{1,0:T(8,128)(2,1)} async-done(((bf16[512,768]{1,0:T(8,128)(2,1)}), bf16[2048,768]{1,0:T(8,128)(2,1)}) %all-gather.2.cloned.1.call-update) | async-done | bytes 3145744 | tf_op jit(solution)/shard_map/all_gather | solution.py:11
  40.2 15.8 %convert_bitcast_fusion = bf16[3,2048,1024]{1,2,0:T(8,128)(2,1)} fusion(bf16[3,768,1024]{2,1,0:T(8,128)(2,1)} %param.9, bf16[2048,768]{1,0:T(8,128)(2,1)} %all-gather.2.cloned.1.call-done), kind=kOutput, calls=%fused_computation.2 | convolution fusion | flops 9669967872 | bytes 20447232 | tf_op jit(solution)/shard_map/nd,rdh->rnh/dot_general | solution.py:12
  56.0 16.7 %copy.14 = bf16[3,2048,1024]{2,1,0:T(8,128)(2,1)} copy(bf16[3,2048,1024]{1,2,0:T(8,128)(2,1)} %convert_bitcast_fusion) | data formatting | bytes 25165824 | tf_op jit(solution)/shard_map/convert_element_type | solution.py:14
  72.6 12.2 %gather_fusion = bf16[64,128,1024]{2,1,0:T(8,128)(2,1)} fusion(bf16[48,128,1024]{2,1,0:T(8,128)(2,1)} %bitcast.31, s32[1024]{0:T(1024)S(1)} %pad_clamp_fusion), kind=kCustom, calls=%fused_computation | custom fusion | bytes 33554688 | tf_op jit(solution)/shard_map/jit(_take)/gather | solution.py:26
  84.8 8.6 %bitcast_select_fusion = bf16[16,512,1024]{2,1,0:T(8,128)(2,1)S(1)} fusion(pred[16,512]{1,0:T(8,128)(4,1)S(1)} %bitcast.35, bf16[16,512,1024]{2,1,0:T(8,128)(2,1)} %bitcast.32), kind=kLoop, calls=%fused_computation.1 | loop fusion | flops 8388608 | bytes 33562624 | tf_op jit(solution)/shard_map/jit(_take)/select_n | solution.py:26
  93.4 7.4 %fusion.4 = f32[16,128,1024]{2,1,0:T(8,128)} fusion(bf16[16,128,512]{1,2,0:T(8,128)(2,1)} %bitcast.34, bf16[16,512,1024]{2,1,0:T(8,128)(2,1)S(1)} %bitcast_select_fusion), kind=kOutput, calls=%fused_computation.15 | convolution fusion | flops 2147483648 | bytes 27262976 | tf_op jit(solution)/shard_map/tij,tjh->tih/dot_general | solution.py:29
  100.7 0.0 copy-start.1
  100.7 0.0 reduce-scatter.2.cloned.1.call-update
  100.7 149.2 %reduce-scatter.2.cloned.1.call-done = f32[256,1024]{1,0:T(8,128)} async-done(((f32[2048,1024]{1,0:T(8,128)}), f32[256,1024]{1,0:T(8,128)}) %reduce-scatter.2.cloned.1.call-update) | async-done | bytes 1048592 | tf_op jit(solution)/shard_map/reduce_scatter | solution.py:33
  249.9 0.0 copy-done
  249.9 0.0 copy-done.1
  249.9 2.6 %fusion.2 = bf16[256,1024]{1,0:T(8,128)(2,1)} fusion(f32[256,1024]{1,0:T(8,128)} %reduce-scatter.2.cloned.1.call-done, bf16[256,768]{1,0:T(8,128)(2,1)S(1)} %copy-done.1, bf16[768,1024]{1,0:T(8,128)(2,1)S(1)} %copy-done), kind=kOutput, calls=%fused_computation.7 | convolution fusion | flops 403439616 | bytes 3538944 | tf_op jit(solution)/shard_map/dot_general | solution.py:34
  (3 shorter events, 0.0 us)
Async XLA Ops:
  6.5 243.4 %copy-start = (bf16[768,1024]{1,0:T(8,128)(2,1)S(1)}, bf16[768,1024]{1,0:T(8,128)(2,1)}, u32[]{:S(2)}) copy-start(bf16[768,1024]{1,0:T(8,128)(2,1)} %param.10) | copy-start | bytes 4718596
  6.5 6.4 %copy-start.2 = (s32[1,16]{1,0:T(1,128)S(1)}, s32[1,16]{1,0:T(1,128)}, u32[]{:S(2)}) copy-start(s32[1,16]{1,0:T(1,128)} %param.13) | copy-start | bytes 196
  6.5 33.6 %all-gather.2.cloned.1.call-start = ((), (), s32[]{:S(2)}) async-start(), calls=%async_computation.1 | async-start | bytes 3932160 | tf_op jit(solution)/shard_map/all_gather | solution.py:11
  7.3 242.6 %reduce-scatter.2.cloned.1.call-start = ((), (), s32[]{:S(2)}) async-start(), calls=%async_computation.2 | async-start | bytes 9437184 | tf_op jit(solution)/shard_map/reduce_scatter | solution.py:33
  100.7 149.2 %copy-start.1 = (bf16[256,768]{1,0:T(8,128)(2,1)S(1)}, bf16[256,768]{1,0:T(8,128)(2,1)}, u32[]{:S(2)}) copy-start(bf16[256,768]{1,0:T(8,128)(2,1)} %param.8) | copy-start | bytes 1179652
Sparse Core Ops, SparseCore 0:
  8.9 31.2 all-gather.1
  100.9 148.9 reduce-scatter.1
where the time goes:
time: 260 us; the launch traced here: 259 us
  waiting for transfers between devices  174 us (67%)
  local copies, waits for them, and re-layouts  33.8 us (13%)
  matrix products  25.7 us (10%)
  between operations  13.4 us (5%)
  other arithmetic  12.5 us (5%)
    reduce_scatter x1, waiting for transfers between devices, shards(): lax.psum_scatter(partial_value, 'src', scatter_dimension=0, tiled=True)  149 us
    all_gather x1, waiting for transfers between devices, shards(): gathered = lax.all_gather(src_feat, 'tgt', axis=0, tiled=True)  24 us
    convert_element_type x1, local copies, waits for them, and re-layouts, shards(): transformed = jnp.einsum('nd,rdh->rnh', gathered, rel_weight, preferred_e...  16.7 us
    dot_general x1, matrix products, shards(): jnp.einsum('nd,rdh->rnh', gathered, rel_weight, preferred_element_type=jn...  15.8 us
    gather x1, local copies, waits for them, and re-layouts, shards(): jnp.take(transformed, source_index.reshape(-1), axis=0)  12.2 us
    select_n x2, other arithmetic, shards(): jnp.take(transformed, source_index.reshape(-1), axis=0)  8.57 us
    dot_general x1, matrix products, shards(): jnp.einsum('tij,tjh->tih', live_weight, picked, preferred_element_type=jn...  7.36 us
  transfers between devices with their start and end apart: 2, of which 2 were waited for; matrix products, arithmetic and copies ran while one was open for 3% of the time, Pallas kernels for 0%

commit v1 on v0

v1 whole, which is shorter than its diff:
```python
import functools

import jax
import jax.numpy as jnp
from jax import lax
from jax.experimental import pallas as pl
from jax.experimental.pallas import tpu as pltpu
from jax.sharding import PartitionSpec as P

BLK = 128
TILE = 256
F32 = jnp.float32
BF16 = jnp.bfloat16


def kernel(n_src, n_tgt, cuts,
           feat, tgt, rel, selfw, adj, index, count, out,
           gath, rel_v, self_v, tgt_v, adj_v, trans, self_acc, peer_msg, own_msg, x_in, up_in, down_in, z_out,
           load_sem, y_send, y_recv, c_send, c_recv, f_send, f_recv, x_send, x_recv, z_send, up_recv, down_recv):
    s, t = lax.axis_index("src"), lax.axis_index("tgt")
    x, z = s % 2, s // 2
    n_z = n_src // 2
    n_y = n_tgt // 2
    mate = t + 1 - 2 * (t % 2)
    x_peer = s + 1 - 2 * x
    rows, rels, hid = gath.shape[1], rel_v.shape[0], rel_v.shape[2]
    per_rel = trans.shape[0] // rels
    tblocks, slots = adj_v.shape[0], adj_v.shape[1]
    pieces, piece = z_out.shape[1], z_out.shape[2]
    owned = pieces * piece
    cut = rows // cuts
    tiles = hid // TILE

    def to(src_ref, dst_ref, send, recv, **where):
        return pltpu.make_async_remote_copy(
            src_ref=src_ref, dst_ref=dst_ref, send_sem=send, recv_sem=recv,
            device_id=where, device_id_type=pl.DeviceIdType.MESH)

    loads = [
        pltpu.make_async_copy(feat, gath.at[t], load_sem.at[0]),
        pltpu.make_async_copy(rel, rel_v, load_sem.at[1]),
        pltpu.make_async_copy(tgt, tgt_v, load_sem.at[2]),
        pltpu.make_async_copy(selfw, self_v, load_sem.at[3]),
        pltpu.make_async_copy(adj.at[0], adj_v, load_sem.at[4]),
    ]
    for load in loads:
        load.start()

    barrier = pltpu.get_barrier_semaphore()

    def greet(**where):
        pl.semaphore_signal(barrier, inc=1, device_id=where, device_id_type=pl.DeviceIdType.MESH)

    greet(tgt=mate)
    greet(src=x_peer)
    for j in range(1, n_y):
        greet(tgt=(t + 2 * j) % n_tgt)
    pl.when(z > 0)(lambda: greet(src=s - 2))
    pl.when(z < n_z - 1)(lambda: greet(src=s + 2))
    pl.semaphore_wait(barrier, n_y + 1 + jnp.minimum(z, 1) + jnp.minimum(n_z - 1 - z, 1))

    def y_copy(j, p, owner, peer):
        spot = pl.ds(p * cut, cut)
        return to(feat.at[spot], gath.at[owner, spot], y_send.at[j - 1, p], y_recv.at[j - 1, p], tgt=peer)

    def f_copy(j, p, owner):
        here = gath.at[owner, pl.ds(p * cut, cut)]
        return to(here, here, f_send.at[j - 1, p], f_recv.at[j - 1, p], tgt=mate)

    for p in range(cuts):
        for j in range(1, n_y):
            y_copy(j, p, t, (t + 2 * j) % n_tgt).start()
    mate_copy = to(feat, gath.at[t], c_send, c_recv, tgt=mate)
    mate_copy.start()

    def transform(owner, first, many):
        block = (owner * rows + first) // BLK

        @pl.loop(0, rels)
        def _(r):
            @pl.loop(0, tiles)
            def _(c):
                col = pl.ds(pl.multiple_of(c * TILE, TILE), TILE)
                made = jnp.dot(gath[owner, pl.ds(first, many), :], rel_v[r, :, col], preferred_element_type=F32)
                trans[pl.ds(r * per_rel + block, many // BLK), :, col] = made.astype(BF16).reshape(many // BLK, BLK, TILE)

    loads[0].wait()
    loads[1].wait()
    transform(t, 0, rows)
    mate_copy.wait_recv()
    transform(mate, 0, rows)
    loads[2].wait()
    loads[3].wait()
    loads[4].wait()

    @pl.loop(0, tiles)
    def _(c):
        col = pl.ds(pl.multiple_of(c * TILE, TILE), TILE)
        made = jnp.dot(tgt_v[...], self_v[:, col], preferred_element_type=F32)
        self_acc[:, :, col] = made.reshape(pieces, piece, TILE)

    for p in range(cuts):
        for j in range(1, n_y):
            owner = (t - 2 * j + n_tgt) % n_tgt
            y_copy(j, p, owner, owner).wait_recv()
            f_copy(j, p, owner).start()
            transform(owner, p * cut, cut)
        for j in range(1, n_y):
            owner = (mate - 2 * j + n_tgt) % n_tgt
            f_copy(j, p, owner).wait_recv()
            transform(owner, p * cut, cut)

    def message(block, store):
        live = [
            (adj_v[block, k].astype(F32) * (k < count[0, block]).astype(F32)).astype(BF16)
            for k in range(slots)
        ]
        left = jnp.concatenate(live, axis=1)
        picks = [index[0, block, k] for k in range(slots)]
        for c in range(tiles):
            col = pl.ds(c * TILE, TILE)
            right = jnp.concatenate([trans[pick, :, col] for pick in picks], axis=0)
            store(col, jnp.dot(left, right, preferred_element_type=F32))

    ups, downs = n_z - 1 - z, z
    both = jnp.minimum(ups, downs)

    def order(i):
        pair = i // 2
        one = jnp.where(i % 2 == 0, n_z - 1 - pair, pair)
        rest = jnp.where(ups > downs, n_z - 1 - i + both, i - both)
        d = jnp.where(i < 2 * both, one, rest)
        return jnp.where(i < n_z - 1, d, z)

    def x_copy(d, p):
        return to(peer_msg.at[d, p], x_in.at[d, p], x_send.at[d, p], x_recv.at[d, p], src=x_peer)

    if owned % BLK == 0:
        def peer_step(i):
            d, p = order(i // pieces), i % pieces

            def store(col, made):
                peer_msg[d, p, :, col] = made.astype(BF16)

            message((d * 2 + 1 - x) * pieces + p, store)
            x_copy(d, p).start()

        def own_step(i):
            d, p = order(i // pieces), i % pieces

            def store(col, made):
                own_msg[d, p, :, col] = made

            message((d * 2 + x) * pieces + p, store)

        pl.loop(0, n_z * pieces)(peer_step)
        pl.loop(0, n_z * pieces)(own_step)
    else:
        share = BLK // owned

        @pl.loop(0, tblocks)
        def _(block):
            def store(col, made):
                for e in range(share):
                    part = made[e * owned:(e + 1) * owned]
                    d = (block * share + e) // 2

                    @pl.when(x == e % 2)
                    def _():
                        own_msg[d, 0, :, col] = part

                    @pl.when(x != e % 2)
                    def _():
                        peer_msg[d, 0, :, col] = part.astype(BF16)

            message(block, store)

        @pl.loop(0, n_z)
        def _(i):
            x_copy(order(i), 0).start()

    def up_copy(d, p):
        return to(z_out.at[d, p], up_in.at[d, p], z_send.at[d, p], up_recv.at[d, p], src=s + 2)

    def down_copy(d, p):
        return to(z_out.at[d, p], down_in.at[d, p], z_send.at[d, p], down_recv.at[d, p], src=s - 2)

    def hop(d, p, copy, arrived, edge):
        x_copy(d, p).wait_recv()

        @pl.when(edge)
        def _():
            z_out[d, p] = (own_msg[d, p] + x_in[d, p].astype(F32)).astype(BF16)

        @pl.when(jnp.logical_not(edge))
        def _():
            copy(d, p).wait_recv()
            z_out[d, p] = (own_msg[d, p] + x_in[d, p].astype(F32) + arrived[d, p].astype(F32)).astype(BF16)

        copy(d, p).start()

    @pl.loop(0, n_z * pieces)
    def _(i):
        k, p = i // pieces, i % pieces
        pl.when(n_z - 1 - k > z)(lambda: hop(n_z - 1 - k, p, up_copy, up_in, z == 0))
        pl.when(k < z)(lambda: hop(k, p, down_copy, down_in, z == n_z - 1))

    @pl.loop(0, pieces)
    def _(p):
        x_copy(z, p).wait_recv()
        self_acc[p] = self_acc[p] + own_msg[z, p] + x_in[z, p].astype(F32)

        @pl.when(z > 0)
        def _():
            up_copy(z, p).wait_recv()
            self_acc[p] = self_acc[p] + up_in[z, p].astype(F32)

        @pl.when(z < n_z - 1)
        def _():
            down_copy(z, p).wait_recv()
            self_acc[p] = self_acc[p] + down_in[z, p].astype(F32)

        out[pl.ds(pl.multiple_of(p * piece, piece), piece), :] = jnp.maximum(self_acc[p], 0.0).astype(BF16)

    mate_copy.wait_send()
    for p in range(cuts):
        for j in range(1, n_y):
            y_copy(j, p, t, mate).wait_send()
            f_copy(j, p, t).wait_send()

    @pl.loop(0, n_z * pieces)
    def _(i):
        d, p = i // pieces, i % pieces
        x_copy(d, p).wait_send()
        pl.when(d != z)(lambda: up_copy(d, p).wait_send())


def shards(n_src, n_tgt, feat, tgt, rel, selfw, adj, index, count):
    rows, depth = feat.shape
    rels, _, hid = rel.shape
    _, tblocks, slots, _, _ = adj.shape
    owned = tgt.shape[0]
    n_z, n_y = n_src // 2, n_tgt // 2
    piece = min(BLK, owned)
    pieces = owned // piece
    cuts = 2
    dma = pltpu.SemaphoreType.DMA
    whole = pl.BlockSpec(memory_space=pl.ANY)
    scalar = pl.BlockSpec(memory_space=pltpu.SMEM)
    held = (n_z, pieces, piece, hid)
    total = n_tgt * rows
    return pl.pallas_call(
        functools.partial(kernel, n_src, n_tgt, cuts),
        out_shape=jax.ShapeDtypeStruct((owned, hid), BF16),
        in_specs=[whole] * 5 + [scalar] * 2,
        out_specs=pl.BlockSpec(memory_space=pltpu.VMEM),
        scratch_shapes=[
            pltpu.VMEM((n_tgt, rows, depth), BF16),
            pltpu.VMEM(rel.shape, BF16),
            pltpu.VMEM(selfw.shape, BF16),
            pltpu.VMEM(tgt.shape, BF16),
            pltpu.VMEM(adj.shape[1:], BF16),
            pltpu.VMEM((rels * total // BLK, BLK, hid), BF16),
            pltpu.VMEM((pieces, piece, hid), F32),
            pltpu.VMEM(held, BF16),
            pltpu.VMEM(held, F32),
            pltpu.VMEM(held, BF16),
            pltpu.VMEM(held, BF16),
            pltpu.VMEM(held, BF16),
            pltpu.VMEM(held, BF16),
            dma((5,)),
            dma((n_y - 1, cuts)), dma((n_y - 1, cuts)),
            dma, dma,
            dma((n_y - 1, cuts)), dma((n_y - 1, cuts)),
            dma((n_z, pieces)), dma((n_z, pieces)),
            dma((n_z, pieces)), dma((n_z, pieces)), dma((n_z, pieces)),
        ],
        compiler_params=pltpu.CompilerParams(
            collective_id=0, has_side_effects=True, vmem_limit_bytes=60 * 2**20),
        cost_estimate=pl.CostEstimate(
            flops=2 * rels * total * depth * hid + 2 * tblocks * slots * BLK * BLK * hid,
            bytes_accessed=2 * (rel.size + adj.size + feat.size), transcendentals=0),
    )(feat, tgt, rel, selfw, adj, index, count)


def solution(mesh):
    return jax.shard_map(
        functools.partial(shards, mesh.shape["src"], mesh.shape["tgt"]),
        mesh=mesh,
        in_specs=(
            P(("src", "tgt"), None),
            P(("tgt", "src"), None),
            P(),
            P(),
            P("src", "tgt", None, None, None),
            P("src", "tgt", None),
            P("src", "tgt"),
        ),
        out_specs=P(("tgt", "src"), None),
        check_vma=False,
    )
```

time: 260 us -> 81.4 us (0.31)
  waiting for transfers between devices: 174 us -> 0 us
  Pallas kernels: 0 us -> 77.9 us
  local copies, waits for them, and re-layouts: 33.8 us -> 3.22 us
  matrix products: 25.7 us -> 0 us
  between operations: 13.4 us -> 0.01 us
  other arithmetic: 12.5 us -> 0 us
    reduce_scatter x1 -> x0, waiting for transfers between devices: 149 us -> none  [shards(): lax.psum_scatter(partial_value, 'src', scatter_dimension=0, tiled=True)]
    pallas_call x0 -> x1, Pallas kernels: none -> 77.9 us  [shards(): pl.pallas_call(functools.partial(kernel, n_src, n_tgt, cuts), out_shape=j...]
    dot_general x3 -> x0, matrix products: 25.7 us -> none  [the longest x1 15.8 us: shards(): jnp.einsum('nd,rdh->rnh', gathered, rel_weight, preferred_element_type=jn...]
    all_gather x1 -> x0, waiting for transfers between devices: 24 us -> none  [shards(): gathered = lax.all_gather(src_feat, 'tgt', axis=0, tiled=True)]
    convert_element_type x1 -> x0, local copies, waits for them, and re-layouts: 16.7 us -> none  [shards(): transformed = jnp.einsum('nd,rdh->rnh', gathered, rel_weight, preferred_e...]
    gather x1 -> x0, local copies, waits for them, and re-layouts: 12.2 us -> none  [shards(): jnp.take(transformed, source_index.reshape(-1), axis=0)]
    select_n x3 -> x0, other arithmetic: 11.7 us -> none  [the longest x2 8.57 us: shards(): jnp.take(transformed, source_index.reshape(-1), axis=0)]
  transfers between devices with their start and end apart: 2 -> 0, of which waited for: 2 -> 0; matrix products, arithmetic and copies ran while one was open for 3% -> 0% of each run, Pallas kernels for 0% -> 0%
where the time goes in v1:
time: 81.4 us; the launch traced here: 81.1 us
  Pallas kernels  77.9 us (96%)
  local copies, waits for them, and re-layouts  3.22 us (4%)
    pallas_call x1, Pallas kernels, shards(): pl.pallas_call(functools.partial(kernel, n_src, n_tgt, cuts), out_shape=j...  77.9 us
    unnamed x2, local copies, waits for them, and re-layouts  3.22 us

profile of v1, /device:TPU:0, one launch (start us, length us, event | category | flops | bytes accessed | tf_op | source)
XLA Modules:
  0.0 81.1 jit_solution(15030130766907107071)
XLA Ops:
  0.0 1.4 %copy.8.index = s32[1,16,4]{2,1,0:T(8,128)} copy(s32[1,16,4]{1,2,0:T(4,128)} %param.12) | data formatting | bytes 512 | tf_op args[5]
  1.4 77.9 %shard_map.73 = bf16[256,1024]{1,0:T(8,128)(2,1)} custom-call(bf16[512,768]{1,0:T(8,128)(2,1)} %feat.1, bf16[256,768]{1,0:T(8,128)(2,1)} %tgt.1, bf16[3,768,1024]{2,1,0:T(8,128)(2,1)} %rel.1, bf16[768,1024]{1,0:T(8,128)(2,1)} %selfw.1, bf16[1,16,4,128,128]{4,3,2,1,0:T(8,128)(2,1)} %adj.1, s32[1,16,4]{2,1,0:T(8,128)} %copy.8.index, s32[1,16]{1,0:T(1,128)} %count.1), custom_call_target="tpu_custom_call" | custom-call | flops 11811160064 | bytes 7602176 | tf_op jit(solution)/shard_map/pallas_call | solution.py:252
  79.3 1.9 %copy.10 = bf16[256,1024]{1,0:T(8,128)(2,1)} copy(bf16[256,1024]{1,0:T(8,128)(2,1)} %shard_map.73) | data formatting | bytes 1048576

commit v2 on v1

v2 whole, which is shorter than its diff:
```python
import functools

import jax
import jax.numpy as jnp
from jax import lax
from jax.experimental import pallas as pl
from jax.experimental.pallas import tpu as pltpu
from jax.sharding import PartitionSpec as P

BLK = 128
TILE = 256
PART = 256
CUTS = 2
F32 = jnp.float32
BF16 = jnp.bfloat16


def kernel(n_src, n_tgt,
           feat, tgt, rel, selfw, adj, index, count, out,
           gath, rel_v, self_v, tgt_v, adj_v, live, trans, self_acc, peer_msg, own_msg, x_in, up_in, down_in, z_out,
           first_up, first_down, first_out,
           load_sem, y_send, y_recv, c_send, c_recv, f_send, f_recv, x_send, x_recv, z_send, up_recv, down_recv,
           first_send, first_up_recv, first_down_recv):
    s, t = lax.axis_index("src"), lax.axis_index("tgt")
    x, z = s % 2, s // 2
    y, core = t // 2, t % 2
    n_z = n_src // 2
    n_y, cuts, _, cut, depth = gath.shape
    mate = t + 1 - 2 * core
    x_peer = s + 1 - 2 * x
    rels, hid = rel_v.shape[0], rel_v.shape[2]
    rows = cuts * cut
    per_rel = trans.shape[0] // rels
    tblocks, slots = adj_v.shape[0], adj_v.shape[1]
    pieces, owned, part = z_out.shape[1], z_out.shape[2], z_out.shape[3]
    tiles = hid // TILE
    halves = TILE // part
    edge = (z == 0) | (z == n_z - 1)

    def to(src_ref, dst_ref, send, recv, **where):
        return pltpu.make_async_remote_copy(
            src_ref=src_ref, dst_ref=dst_ref, send_sem=send, recv_sem=recv,
            device_id=where, device_id_type=pl.DeviceIdType.MESH)

    def features(p):
        return feat.at[pl.ds(p * cut, cut)]

    loads = [
        pltpu.make_async_copy(rel, rel_v, load_sem.at[0]),
        pltpu.make_async_copy(tgt, tgt_v, load_sem.at[1]),
        pltpu.make_async_copy(selfw, self_v, load_sem.at[2]),
        pltpu.make_async_copy(adj.at[0], adj_v, load_sem.at[3]),
    ] + [
        pltpu.make_async_copy(features(p), gath.at[y, p, core], load_sem.at[4 + p])
        for p in range(cuts)
    ]
    for load in loads:
        load.start()

    barrier = pltpu.get_barrier_semaphore()

    def greet(**where):
        pl.semaphore_signal(barrier, inc=1, device_id=where, device_id_type=pl.DeviceIdType.MESH)

    greet(tgt=mate)
    greet(src=x_peer)
    for j in range(1, n_y):
        greet(tgt=(t + 2 * j) % n_tgt)
    pl.when(z > 0)(lambda: greet(src=s - 2))
    pl.when(z < n_z - 1)(lambda: greet(src=s + 2))
    pl.semaphore_wait(barrier, n_y + 1 + jnp.minimum(z, 1) + jnp.minimum(n_z - 1 - z, 1))

    def y_copy(j, p, owner, peer):
        return to(features(p), gath.at[owner, p, core], y_send.at[j - 1, p], y_recv.at[j - 1, p], tgt=peer)

    def f_copy(j, p, owner):
        here = gath.at[owner, p, core]
        return to(here, here, f_send.at[j - 1, p], f_recv.at[j - 1, p], tgt=mate)

    def mate_copy(p):
        return to(features(p), gath.at[y, p, core], c_send.at[p], c_recv.at[p], tgt=mate)

    for p in range(cuts):
        for j in range(1, n_y):
            y_copy(j, p, y, (t + 2 * j) % n_tgt).start()
    for p in range(cuts):
        mate_copy(p).start()

    def transform(owner, p, c):
        col = pl.ds(pl.multiple_of(c * TILE, TILE), TILE)
        many = cut // BLK
        block = (2 * owner * rows + p * cut) // BLK
        for r in range(rels):
            made = jnp.dot(gath[owner, p].reshape(2 * cut, depth), rel_v[r, :, col], preferred_element_type=F32)
            made = made.astype(BF16).reshape(2, many, BLK, TILE)
            trans[pl.ds(r * per_rel + block, many), :, col] = made[0]
            trans[pl.ds(r * per_rel + block + rows // BLK, many), :, col] = made[1]

    loads[0].wait()
    for p in range(cuts):
        loads[4 + p].wait()
        mate_copy(p).wait_recv()
        pl.loop(0, tiles)(lambda c: transform(y, p, c))
    for load in loads[1:4]:
        load.wait()

    @pl.loop(0, tiles)
    def _(c):
        col = pl.ds(pl.multiple_of(c * TILE, TILE), TILE)
        made = jnp.dot(tgt_v[...], self_v[:, col], preferred_element_type=F32)
        for h in range(halves):
            self_acc[c * halves + h] = made[:, h * part:(h + 1) * part]

    @pl.loop(0, tblocks)
    def _(block):
        for k in range(slots):
            keep = (k < count[0, block]).astype(F32)
            live[block, :, k * BLK:(k + 1) * BLK] = (adj_v[block, k].astype(F32) * keep).astype(BF16)

    def arrive(p):
        for j in range(1, n_y):
            owner = (y - j + n_y) % n_y
            y_copy(j, p, owner, t).wait_recv()
            f_copy(j, p, owner).start()
        for j in range(1, n_y):
            f_copy(j, p, (y - j + n_y) % n_y).wait_recv()

    for p in range(cuts - 1):
        arrive(p)
        for j in range(1, n_y):
            pl.loop(0, tiles)(lambda c: transform((y - j + n_y) % n_y, p, c))
    arrive(cuts - 1)

    def message(block, c):
        col = pl.ds(pl.multiple_of(c * TILE, TILE), TILE)
        right = jnp.concatenate([trans[index[0, block, k], :, col] for k in range(slots)], axis=0)
        return jnp.dot(live[block], right, preferred_element_type=F32)

    ups, downs = n_z - 1 - z, z
    both = jnp.minimum(ups, downs)

    def order(i):
        pair = i // 2
        one = jnp.where(i % 2 == 0, n_z - 1 - pair, pair)
        rest = jnp.where(ups > downs, n_z - 1 - i + both, i - both)
        d = jnp.where(i < 2 * both, one, rest)
        return jnp.where(i < n_z - 1, d, z)

    def x_copy(d, p):
        return to(peer_msg.at[d, p], x_in.at[d, p], x_send.at[d, p], x_recv.at[d, p], src=x_peer)

    def first_copy(d, side, way):
        here = first_out.at[d, side]
        if way == 0:
            return to(here, first_up.at[d, side], first_send.at[d, side], first_up_recv.at[d, side], src=s + 2)
        return to(here, first_down.at[d, side], first_send.at[d, side], first_down_recv.at[d, side], src=s - 2)

    def start_x(d, c):
        for h in range(halves):
            p = c * halves + h
            pl.when(p > 0)(lambda: x_copy(d, p).start())

    def aggregate(c):
        if owned % BLK == 0:
            many = owned // BLK

            def build(d, side, place):
                for b in range(many):
                    made = message((d * 2 + side) * many + b, c)
                    for h in range(halves):
                        got = made[:, h * part:(h + 1) * part].astype(place.dtype)
                        place[d, c * halves + h, b * BLK:(b + 1) * BLK, :] = got

            @pl.loop(0, n_z)
            def _(i):
                d = order(i)
                build(d, 1 - x, peer_msg)
                start_x(d, c)

            pl.loop(0, n_z)(lambda i: build(order(i), x, own_msg))
        else:
            share = BLK // owned

            @pl.loop(0, tblocks)
            def _(block):
                made = message(block, c)
                for e in range(share):
                    d = (block * share + e) // 2
                    for h in range(halves):
                        got = made[e * owned:(e + 1) * owned, h * part:(h + 1) * part]

                        @pl.when(x == e % 2)
                        def _():
                            own_msg[d, c * halves + h] = got

                        @pl.when(x != e % 2)
                        def _():
                            peer_msg[d, c * halves + h] = got.astype(BF16)

            pl.loop(0, n_z)(lambda i: start_x(order(i), c))

    @pl.loop(0, tiles)
    def _(c):
        for j in range(1, n_y):
            transform((y - j + n_y) % n_y, cuts - 1, c)
        aggregate(c)

        @pl.when((c == 0) & edge)
        def _():
            @pl.loop(0, n_z - 1)
            def _(i):
                d = order(i)
                first_out[d, 0] = own_msg[d, 0].astype(BF16)
                first_out[d, 1] = peer_msg[d, 0]
                for side in range(2):
                    pl.when(z == 0)(lambda: first_copy(d, side, 0).start())
                    pl.when(z > 0)(lambda: first_copy(d, side, 1).start())

    def first_hop(d, way, arrived):
        for side, held in ((0, own_msg), (1, peer_msg)):
            copy = first_copy(d, side, way)
            copy.wait_recv()
            first_out[d, side] = (held[d, 0].astype(F32) + arrived[d, side].astype(F32)).astype(BF16)
            copy.start()

    def up_copy(d, p):
        return to(z_out.at[d, p], up_in.at[d, p], z_send.at[d, p], up_recv.at[d, p], src=s + 2)

    def down_copy(d, p):
        return to(z_out.at[d, p], down_in.at[d, p], z_send.at[d, p], down_recv.at[d, p], src=s - 2)

    def hop(d, p, copy, arrived, last):
        x_copy(d, p).wait_recv()

        @pl.when(last)
        def _():
            z_out[d, p] = (own_msg[d, p] + x_in[d, p].astype(F32)).astype(BF16)

        @pl.when(jnp.logical_not(last))
        def _():
            copy(d, p).wait_recv()
            z_out[d, p] = (own_msg[d, p] + x_in[d, p].astype(F32) + arrived[d, p].astype(F32)).astype(BF16)

        copy(d, p).start()

    def finish(p, total):
        total = total + x_in[z, p].astype(F32)
        out[:, pl.ds(pl.multiple_of(p * part, part), part)] = jnp.maximum(total, 0.0).astype(BF16)

    def close(p):
        self_acc[p] = self_acc[p] + own_msg[z, p]

        @pl.when(z > 0)
        def _():
            up_copy(z, p).wait_recv()
            self_acc[p] = self_acc[p] + up_in[z, p].astype(F32)

        @pl.when(z < n_z - 1)
        def _():
            down_copy(z, p).wait_recv()
            self_acc[p] = self_acc[p] + down_in[z, p].astype(F32)

        x_copy(z, p).wait_recv()
        finish(p, self_acc[p])

    def cross():
        self_acc[0] = self_acc[0] + own_msg[z, 0]
        own_msg[z, 0] = peer_msg[z, 0].astype(F32)
        for reached, way, arrived in ((z > 0, 0, first_up), (z < n_z - 1, 1, first_down)):
            @pl.when(reached)
            def _():
                for side in range(2):
                    first_copy(z, side, way).wait_recv()
                self_acc[0] = self_acc[0] + arrived[z, 0].astype(F32)
                own_msg[z, 0] = own_msg[z, 0] + arrived[z, 1].astype(F32)
        peer_msg[z, 0] = own_msg[z, 0].astype(BF16)
        x_copy(z, 0).start()

    @pl.loop(0, pieces + n_z)
    def _(i):
        up, down = i - z, i - (n_z - 1 - z)

        @pl.loop(0, n_z)
        def _(k):
            far = n_z - 1 - k

            @pl.when(far > z)
            def _():
                pl.when((up == 0) & jnp.logical_not(edge))(lambda: first_hop(far, 0, first_up))
                pl.when((up > 0) & (up < pieces))(lambda: hop(far, up, up_copy, up_in, z == 0))

            @pl.when(k < z)
            def _():
                pl.when((down == 0) & jnp.logical_not(edge))(lambda: first_hop(k, 1, first_down))
                pl.when((down > 0) & (down < pieces))(lambda: hop(k, down, down_copy, down_in, z == n_z - 1))

        pl.when(i == n_z)(cross)
        pl.when(i > n_z)(lambda: close(i - n_z))

    x_copy(z, 0).wait_recv()
    finish(0, self_acc[0])

    for p in range(cuts):
        mate_copy(p).wait_send()
        for j in range(1, n_y):
            y_copy(j, p, y, mate).wait_send()
            f_copy(j, p, y).wait_send()

    @pl.loop(0, n_z)
    def _(d):
        @pl.when(d != z)
        def _():
            for side in range(2):
                first_copy(d, side, 0).wait_send()

        pl.when(d == z)(lambda: x_copy(d, 0).wait_send())

        @pl.loop(1, pieces)
        def _(p):
            x_copy(d, p).wait_send()
            pl.when(d != z)(lambda: up_copy(d, p).wait_send())


def shards(n_src, n_tgt, feat, tgt, rel, selfw, adj, index, count):
    rows, depth = feat.shape
    rels, _, hid = rel.shape
    _, tblocks, slots, _, _ = adj.shape
    owned = tgt.shape[0]
    n_z, n_y = n_src // 2, n_tgt // 2
    pieces = hid // PART
    cuts = CUTS
    dma = pltpu.SemaphoreType.DMA
    whole = pl.BlockSpec(memory_space=pl.ANY)
    scalar = pl.BlockSpec(memory_space=pltpu.SMEM)
    held = (n_z, pieces, owned, PART)
    first = (n_z, 2, owned, PART)
    total = n_tgt * rows
    return pl.pallas_call(
        functools.partial(kernel, n_src, n_tgt),
        out_shape=jax.ShapeDtypeStruct((owned, hid), BF16),
        in_specs=[whole] * 5 + [scalar] * 2,
        out_specs=pl.BlockSpec(memory_space=pltpu.VMEM),
        scratch_shapes=[
            pltpu.VMEM((n_y, cuts, 2, rows // cuts, depth), BF16),
            pltpu.VMEM(rel.shape, BF16),
            pltpu.VMEM(selfw.shape, BF16),
            pltpu.VMEM(tgt.shape, BF16),
            pltpu.VMEM(adj.shape[1:], BF16),
            pltpu.VMEM((tblocks, BLK, slots * BLK), BF16),
            pltpu.VMEM((rels * total // BLK, BLK, hid), BF16),
            pltpu.VMEM((pieces, owned, PART), F32),
            pltpu.VMEM(held, BF16),
            pltpu.VMEM(held, F32),
            pltpu.VMEM(held, BF16),
            pltpu.VMEM(held, BF16),
            pltpu.VMEM(held, BF16),
            pltpu.VMEM(held, BF16),
            pltpu.VMEM(first, BF16),
            pltpu.VMEM(first, BF16),
            pltpu.VMEM(first, BF16),
            dma((4 + cuts,)),
            dma((n_y - 1, cuts)), dma((n_y - 1, cuts)),
            dma((cuts,)), dma((cuts,)),
            dma((n_y - 1, cuts)), dma((n_y - 1, cuts)),
            dma((n_z, pieces)), dma((n_z, pieces)),
            dma((n_z, pieces)), dma((n_z, pieces)), dma((n_z, pieces)),
            dma((n_z, 2)), dma((n_z, 2)), dma((n_z, 2)),
        ],
        compiler_params=pltpu.CompilerParams(
            collective_id=0, has_side_effects=True, vmem_limit_bytes=60 * 2**20),
        cost_estimate=pl.CostEstimate(
            flops=2 * rels * total * depth * hid + 2 * tblocks * slots * BLK * BLK * hid,
            bytes_accessed=2 * (rel.size + adj.size + feat.size), transcendentals=0),
    )(feat, tgt, rel, selfw, adj, index, count)


def solution(mesh):
    return jax.shard_map(
        functools.partial(shards, mesh.shape["src"], mesh.shape["tgt"]),
        mesh=mesh,
        in_specs=(
            P(("src", "tgt"), None),
            P(("tgt", "src"), None),
            P(),
            P(),
            P("src", "tgt", None, None, None),
            P("src", "tgt", None),
            P("src", "tgt"),
        ),
        out_specs=P(("tgt", "src"), None),
        check_vma=False,
    )
```

time: 81.4 us -> 80.6 us (level)
    pallas_call x1, Pallas kernels: 77.9 us -> 77.1 us  [shards(): pl.pallas_call(functools.partial(kernel, n_src, n_tgt), out_shape=jax.Sha...]
where the time goes in v2:
time: 80.6 us; the launch traced here: 80.3 us
  Pallas kernels  77.1 us (96%)
  local copies, waits for them, and re-layouts  3.22 us (4%)
    pallas_call x1, Pallas kernels, shards(): pl.pallas_call(functools.partial(kernel, n_src, n_tgt), out_shape=jax.Sha...  77.1 us
    unnamed x2, local copies, waits for them, and re-layouts  3.22 us

profile of v2, /device:TPU:0, one launch (start us, length us, event | category | flops | bytes accessed | tf_op | source)
XLA Modules:
  0.0 80.3 jit_solution(2361124024379086593)
XLA Ops:
  0.0 1.4 %copy.8.index = s32[1,16,4]{2,1,0:T(8,128)} copy(s32[1,16,4]{1,2,0:T(4,128)} %param.12) | data formatting | bytes 512 | tf_op args[5]
  1.4 77.1 %shard_map.73 = bf16[256,1024]{1,0:T(8,128)(2,1)} custom-call(bf16[512,768]{1,0:T(8,128)(2,1)} %feat.1, bf16[256,768]{1,0:T(8,128)(2,1)} %tgt.1, bf16[3,768,1024]{2,1,0:T(8,128)(2,1)} %rel.1, bf16[768,1024]{1,0:T(8,128)(2,1)} %selfw.1, bf16[1,16,4,128,128]{4,3,2,1,0:T(8,128)(2,1)} %adj.1, s32[1,16,4]{2,1,0:T(8,128)} %copy.8.index, s32[1,16]{1,0:T(1,128)} %count.1), custom_call_target="tpu_custom_call" | custom-call | flops 11811160064 | bytes 7602176 | tf_op jit(solution)/shard_map/pallas_call | solution.py:338
  78.5 1.9 %copy.10 = bf16[256,1024]{1,0:T(8,128)(2,1)} copy(bf16[256,1024]{1,0:T(8,128)(2,1)} %shard_map.73) | data formatting | bytes 1048576
